TPU v7x, 32 devices: a whole 2x2x4 slice. The times are simulated.
32 devices in a mesh: seq: 16 (over z, x, core), head: 2 (over y).
Axes of the slice: x: 2, y: 2, z: 4, core: 2. Of those that a mesh axis runs over, the one named last changes fastest.
Arguments:
- queries: bfloat16 [2048, 2560], P('seq', 'head'), may hold values from -6 to 6
- keys: bfloat16 [2048, 2560], P('seq', 'head'), may hold values from -6 to 6
- values: bfloat16 [2048, 2560], P('seq', 'head'), may hold values from -6 to 6
- grad_out: bfloat16 [2048, 2560], P('seq', 'head'), may hold values from -6 to 6
- cache: bfloat16 [2048, 2560], P('seq', 'head'), may hold values from -6 to 6
- w_kv: bfloat16 [2, 2560, 2560], P(None, 'seq', 'head'), may hold values from -0.125 to 0.125
- doc_ids: int32 [2048], replicated, may hold values from 0 to 15, never falling along the last dimension, each value on 1 to 256 neighbouring positions
- routes: int32 [2048], replicated, may hold values from 0 to 15, as said below
Outputs:
- output: bfloat16 [2048, 2560], P('seq', 'head')
- grad_q: bfloat16 [2048, 2560], P('seq', 'head')
- grad_k: bfloat16 [2048, 2560], P('seq', 'head')
- grad_v: bfloat16 [2048, 2560], P('seq', 'head')
Inputs may be any that keep to these rules, and one draw needn't show every extreme that they name: `routes`: each device's aligned block of 128 rows names every destination at most 16 times; in every draw some destination is named exactly 16 times by every block.
All inputs are finite; a program needn't handle non-finite values.
Results may differ from a plain program's by a relative error of at most 0.03.
Values may be sent and summed in bfloat16 or wider, within the bound.
No kernel may reach another device: no remote copies, remote signals or barrier semaphores. Data moves between devices by JAX's collectives and lax.ppermute only.
A program may use at most 128 MiB of HBM per device.

v0:
```python
import functools

import jax
import jax.numpy as jnp
from jax import lax
from jax.experimental import pallas as pl
from jax.experimental.pallas import tpu as pltpu
from jax.sharding import Mesh, PartitionSpec as P

HD = 128
SPAN = 2
GROUPS = 4
SEQ = ("z", "p")
ROW_TILE = 16
RING = [0, 1, 3, 2]
VMEM = 60 * 1024 * 1024


def shifted(value, by):
    length = lax.axis_size("z") * lax.axis_size("p")
    pairs = [(i, i + by) for i in range(length) if 0 <= i + by < length]
    return lax.ppermute(value, SEQ, pairs)


def swapped(value, axis, mask):
    return lax.ppermute(value, axis, [(i, i ^ mask) for i in range(lax.axis_size(axis))])


def dot_t(a, b, dims):
    return lax.dot_general(a, b, (dims, ((), ())), preferred_element_type=jnp.float32)


def attend_kernel(
    q_ref, g_ref, k_ref, v_ref, kv1_ref, kv2_ref, mem_ref, bias_ref, *refs
):
    out_ref, gq_ref, far_ref, near_ref, own_ref = refs[-5:]
    rows, width = q_ref.shape
    slots = mem_ref.shape[1]
    scaling = HD ** (-0.5)
    bias = bias_ref[...]
    heads = [slice(i * HD, (i + 1) * HD) for i in range(width // HD)]
    ks = [
        jnp.concatenate(
            [mem_ref[0, :, cols], kv2_ref[0, :, cols], kv1_ref[0, :, cols], k_ref[:, cols]], 0
        )
        for cols in heads
    ]
    vs = [
        jnp.concatenate(
            [mem_ref[1, :, cols], kv2_ref[1, :, cols], kv1_ref[1, :, cols], v_ref[:, cols]], 0
        )
        for cols in heads
    ]
    scores = [dot_t(q_ref[:, cols], kh, ((1,), (1,))) + bias for cols, kh in zip(heads, ks)]
    dprobs = [dot_t(g_ref[:, cols], vh, ((1,), (1,))) for cols, vh in zip(heads, vs)]
    probs = []
    for score in scores:
        weights = jnp.exp((score - jnp.max(score, axis=-1, keepdims=True)) * scaling)
        probs.append(weights * (1.0 / jnp.sum(weights, axis=-1, keepdims=True)))
    probs_b = [prob.astype(jnp.bfloat16) for prob in probs]
    outs = [
        dot_t(prob_b, vh, ((1,), (0,))).astype(jnp.bfloat16) for prob_b, vh in zip(probs_b, vs)
    ]
    dscores = []
    for cols, out_b, prob, dprob in zip(heads, outs, probs, dprobs):
        out_ref[:, cols] = out_b
        delta = jnp.sum(
            g_ref[:, cols].astype(jnp.float32) * out_b.astype(jnp.float32), axis=-1, keepdims=True
        )
        dscores.append((prob * ((dprob - delta) * scaling)).astype(jnp.bfloat16))
    for cols, kh, dscore, prob_b in zip(heads, ks, dscores, probs_b):
        gq_ref[:, cols] = dot_t(dscore, kh, ((1,), (0,))).astype(jnp.bfloat16)
        grad_k = dot_t(dscore[:, slots:], q_ref[:, cols], ((0,), (0,)))
        grad_v = dot_t(prob_b[:, slots:], g_ref[:, cols], ((0,), (0,)))
        for i, grad in enumerate((grad_k, grad_v)):
            far_ref[i, :, cols] = grad[:rows].astype(jnp.bfloat16)
            near_ref[i, :, cols] = grad[rows : 2 * rows]
            own_ref[i, :, cols] = grad[2 * rows :]


def attend(first, queries, grad_out, keys, values, kv1, kv2, memory, bias, earlier):
    rows, features = queries.shape
    steps = memory.shape[0] // 2
    slots, block = memory.shape[1:]
    heads = steps * block // HD
    offset = first // block
    flat = pl.BlockSpec((rows, block), lambda i: (0, i + offset))
    pair = pl.BlockSpec((2, rows, block), lambda i: (0, 0, i + offset))
    grad = pl.BlockSpec((2, rows, block), lambda i: (0, 0, i))
    whole = pl.BlockSpec(memory_space=pl.ANY)
    keys_all = slots + 3 * rows
    return pl.pallas_call(
        attend_kernel,
        grid=(steps,),
        in_specs=[
            flat, flat, flat, flat, pair, pair,
            pl.BlockSpec((2, slots, block), lambda i: (i, 0, 0)),
            pl.BlockSpec((rows, keys_all), lambda i: (0, 0)),
            *([whole] * len(earlier)),
        ],
        out_specs=[flat, flat, grad, grad, grad],
        out_shape=[
            jax.ShapeDtypeStruct((rows, features), jnp.bfloat16),
            jax.ShapeDtypeStruct((rows, features), jnp.bfloat16),
            jax.ShapeDtypeStruct((2, rows, steps * block), jnp.bfloat16),
            jax.ShapeDtypeStruct((2, rows, steps * block), jnp.float32),
            jax.ShapeDtypeStruct((2, rows, steps * block), jnp.float32),
        ],
        input_output_aliases={8 + i: i for i in range(len(earlier))},
        compiler_params=pltpu.CompilerParams(vmem_limit_bytes=VMEM),
        cost_estimate=pl.CostEstimate(
            flops=2 * 5 * rows * keys_all * HD * heads,
            bytes_accessed=8 * 1024 * 1024,
            transcendentals=rows * keys_all * heads,
        ),
        name="attend",
    )(queries, grad_out, keys, values, kv1, kv2, memory, bias, *earlier)


def project_kernel(first, order_ref, place_ref, *refs):
    n_z = place_ref.shape[0]
    out_ref, w_ref, a_ref, sems = refs[-4:]
    rows = refs[: 2 * n_z]
    pieces = refs[2 * n_z : -4]
    n_p, w_rows, block = len(pieces), w_ref.shape[2], w_ref.shape[3]
    depth = rows[0].shape[1]
    cache_rows = place_ref.shape[2]
    devices, _, capacity, _ = out_ref.shape
    copies = []
    for i, ref in enumerate(rows):
        start = pl.multiple_of(order_ref[n_z + n_p + i // n_z] * depth, HD)
        to = a_ref.at[order_ref[n_z + n_p + 2 + i % n_z], :, pl.ds(start, depth)]
        copies.append(pltpu.make_async_copy(ref, to, sems.at[len(copies)]))
    for m in range(n_p):
        for k in range(n_z):
            copies.append(
                pltpu.make_async_copy(
                    pieces[m].at[k, :, pl.ds(first, block)],
                    w_ref.at[order_ref[k], order_ref[n_z + m]],
                    sems.at[len(copies)],
                )
            )
    for copy in copies:
        copy.start()
    for copy in copies:
        copy.wait()
    a = a_ref[...].reshape(n_z * cache_rows, 2 * depth)
    w = w_ref[...].reshape(2 * depth, block)
    proj = jnp.dot(a, w, preferred_element_type=jnp.float32).astype(jnp.bfloat16)
    slot_ids = lax.broadcasted_iota(jnp.int32, (devices * capacity, cache_rows), 0)
    for z in range(n_z):
        chosen = jnp.where(slot_ids == place_ref[z], 1.0, 0.0).astype(jnp.bfloat16)
        slots = jnp.dot(
            chosen,
            proj[z * cache_rows : (z + 1) * cache_rows],
            preferred_element_type=jnp.float32,
        ).astype(jnp.bfloat16)
        out_ref[:, z] = slots.reshape(devices, capacity, block)


def project(first, block, order, place, rows, pieces, devices, capacity):
    n_z, _, cache_rows = place.shape
    depth = rows[0].shape[1]
    n_p = len(pieces)
    w_rows = pieces[0].shape[1]
    whole = pl.BlockSpec(memory_space=pl.ANY)
    return pl.pallas_call(
        functools.partial(project_kernel, first),
        in_specs=[
            pl.BlockSpec(memory_space=pltpu.SMEM),
            pl.BlockSpec(memory_space=pltpu.VMEM),
            *([whole] * (len(rows) + n_p)),
        ],
        out_specs=pl.BlockSpec(memory_space=pltpu.VMEM),
        out_shape=jax.ShapeDtypeStruct((devices, n_z, capacity, block), jnp.bfloat16),
        scratch_shapes=[
            pltpu.VMEM((n_z, n_p, w_rows, block), jnp.bfloat16),
            pltpu.VMEM((n_z, cache_rows, 2 * depth), jnp.bfloat16),
            pltpu.SemaphoreType.DMA((n_p * n_z + len(rows),)),
        ],
        compiler_params=pltpu.CompilerParams(vmem_limit_bytes=VMEM),
        cost_estimate=pl.CostEstimate(
            flops=4 * n_z * cache_rows * depth * block,
            bytes_accessed=8 * 1024 * 1024,
            transcendentals=0,
        ),
        name="project",
    )(order, place, *rows, *pieces)


def slot_places(routes, n_z, n_p, cache_rows, capacity):
    mine = lax.dynamic_index_in_dim(
        routes.reshape(n_z, n_p, cache_rows), lax.axis_index("p"), 1, keepdims=False
    )
    ids = jnp.arange(cache_rows, dtype=jnp.int32)
    same = mine[:, :, None] == mine[:, None, :]
    ranks = jnp.sum((same & (ids[None, :] < ids[:, None])[None]).astype(jnp.int32), axis=2)
    return mine * capacity + ranks


def widths(features):
    heads = features // HD // 2
    first = (heads + 1) // 2
    return (first * HD, (heads - first) * HD)


def column_block(w_kv, target):
    parts, offset = [], 0
    for width in widths(w_kv.shape[2]):
        start = (target & 1, 0, offset + (target >> 1) * width)
        parts.append(lax.dynamic_slice(w_kv, start, (1, w_kv.shape[1], width))[0])
        offset += 2 * width
    return jnp.concatenate(parts, 1)


def ring_step(value):
    return lax.ppermute(value, "z", [(a, b) for a, b in zip(RING, RING[1:] + RING[:1])])


def memory_slots(cache, w_kv, place, capacity, stream):
    n_z, n_p = lax.axis_size("z"), lax.axis_size("p")
    devices = n_z * n_p
    cache_rows, depth = cache.shape
    _, w_rows, features = w_kv.shape
    z, p, y = lax.axis_index("z"), lax.axis_index("p"), lax.axis_index("head")
    chunks = widths(features)
    if n_p == 4 and capacity % ROW_TILE == 0 and w_rows % ROW_TILE == 0:
        blocks = [column_block(w_kv, z ^ mask) for mask in range(n_z)]
        own = jnp.stack(
            [blocks[0]] + [swapped(blocks[mask], "z", mask) for mask in range(1, n_z)], 0
        )
        row1, other0, near = ring_step(cache), swapped(cache, "head", 1), shifted(stream, 1)
        own, row1, other0, near = lax.optimization_barrier((own, row1, other0, near))
        across = swapped(own, "p", 2)
        beside = swapped(own, "p", 1)
        row2, other1 = ring_step(row1), swapped(row1, "head", 1)
        row2, other1, beside = lax.optimization_barrier((row2, other1, beside))
        row3, other2 = ring_step(row2), swapped(row2, "head", 1)
        across, near = lax.optimization_barrier((across, near))
        pieces = [own, beside, across, swapped(across, "p", 1)]
        far = shifted(near, 1)
        rows = [cache, row1, row2, row3, other0, other1, other2, swapped(row3, "head", 1)]
        sources = jnp.asarray(
            [[RING[(RING.index(i) - r) % n_z] for r in range(n_z)] for i in range(n_z)], jnp.int32
        )
        order = jnp.concatenate(
            [z ^ jnp.arange(n_z), p ^ jnp.arange(n_p), jnp.stack([y, 1 - y]), sources[z]]
        ).astype(jnp.int32)
        place, near, far = lax.optimization_barrier((place, near, far))
        place = place.reshape(n_z, 1, cache_rows)
        slots, first = [], 0
        for width in chunks:
            slots.append(project(first, width, order, place, rows, pieces, devices, capacity))
            first += width
        return slots, near, far
    near = shifted(stream, 1)
    far = shifted(near, 1)
    targets = [column_block(w_kv, jnp.int32(i)) for i in range(n_z)]
    w_z = lax.all_to_all(jnp.stack(targets, 0), "z", split_axis=0, concat_axis=0, tiled=True)
    w_all = lax.all_gather(w_z, "p", axis=1, tiled=True).reshape(devices * w_rows, -1)
    rows = lax.all_gather(cache, ("head", "z"), axis=0, tiled=False)
    rows = rows.reshape(-1, n_z * cache_rows, depth)
    proj = sum(
        jnp.dot(
            rows[i], w_all[i * depth : (i + 1) * depth], preferred_element_type=jnp.float32
        )
        for i in range(rows.shape[0])
    ).astype(jnp.bfloat16)
    slot_ids = jnp.arange(devices * capacity, dtype=jnp.int32)
    chosen = (slot_ids[None, :, None] == place[:, None, :]).astype(jnp.bfloat16)
    slots = jnp.einsum(
        "zsi,zic->zsc",
        chosen,
        proj.reshape(n_z, cache_rows, -1),
        preferred_element_type=jnp.float32,
    ).astype(jnp.bfloat16)
    slots = slots.reshape(n_z, devices, capacity, -1).transpose(1, 0, 2, 3)
    return [slots[..., : chunks[0]], slots[..., chunks[0] :]], near, far


def body(queries, keys, values, grad_out, cache, w_kv, doc_ids, routes):
    n_z, n_p = lax.axis_size("z"), lax.axis_size("p")
    devices = n_z * n_p
    my_index = lax.axis_index(SEQ)
    seg_rows = queries.shape[0]
    cache_rows = cache.shape[0]
    capacity = 2 * cache_rows // devices
    slot_count = capacity * devices
    pad_rows = SPAN * seg_rows
    window = pad_rows + seg_rows

    place = slot_places(routes, n_z, n_p, cache_rows, capacity)
    slots, kv1, kv2 = memory_slots(cache, w_kv, place, capacity, jnp.stack([keys, values], 0))
    memory = [
        lax.all_to_all(part, SEQ, split_axis=0, concat_axis=0, tiled=True).reshape(
            n_z, slot_count, part.shape[-1]
        )
        for part in slots
    ]

    incoming = jnp.sum(
        (routes.reshape(n_z, n_p, cache_rows) == my_index).astype(jnp.int32), axis=2
    ).T
    live = jnp.arange(capacity, dtype=jnp.int32)[None, None, :] < incoming[:, :, None]
    live = live.reshape(slot_count)
    start = my_index * seg_rows
    id_pad = jnp.concatenate([jnp.full((pad_rows,), -1, jnp.int32), doc_ids])
    q_ids = lax.dynamic_slice_in_dim(doc_ids, start, seg_rows)
    k_ids = lax.dynamic_slice_in_dim(id_pad, start, window)
    q_pos = start + jnp.arange(seg_rows, dtype=jnp.int32)
    k_pos = start - pad_rows + jnp.arange(window, dtype=jnp.int32)
    allowed_win = (k_pos[None, :] <= q_pos[:, None]) & (k_ids[None, :] == q_ids[:, None])
    allowed = jnp.concatenate(
        [jnp.broadcast_to(live[None, :], (seg_rows, slot_count)), allowed_win], 1
    )
    bias = jnp.where(allowed, 0.0, -1e30).astype(jnp.float32)

    first, earlier, grads = 0, [], []
    for part in memory:
        output, grad_q, far, near, own = attend(
            first, queries, grad_out, keys, values, kv1, kv2, part, bias, earlier
        )
        earlier = [output, grad_q]
        first += 2 * part.shape[-1]
        near = shifted(far, -1).astype(jnp.float32) + near
        own = shifted(near.astype(jnp.bfloat16), -1).astype(jnp.float32) + own
        grads.append(own.astype(jnp.bfloat16))
    grad_k, grad_v = (jnp.concatenate([part[i] for part in grads], 1) for i in range(2))
    return (output, grad_q, grad_k, grad_v)


def solution(mesh):
    n_seq, n_head = mesh.devices.shape
    grid = Mesh(mesh.devices.reshape(GROUPS, n_seq // GROUPS, n_head), ("z", "p", "head"))
    rows = P(SEQ, "head")
    return jax.shard_map(
        body,
        mesh=grid,
        in_specs=(rows, rows, rows, rows, rows, P(None, SEQ, "head"), P(), P()),
        out_specs=(rows, rows, rows, rows),
        check_vma=False,
    )
```

profile of v0, /device:TPU:16, one launch (start us, length us, event | category | flops | bytes accessed | tf_op | source)
XLA Modules:
  0.0 154.3 jit_solution(17122576045778508754)
XLA Ops:
  0.6 1.2 pad_maximum_fusion.1
  1.9 1.9 %collective-permute-start.5 = (bf16[2,128,1280]{2,1,0:T(8,128)(2,1)S(1)}, bf16[2,128,1280]{2,1,0:T(8,128)(2,1)}, u32[]{:S(2)}, u32[]{:S(2)}) collective-permute-start(bf16[2,128,1280]{2,1,0:T(8,128)(2,1)S(1)} %pad_maximum_fusion.1), channel_id=1, source_target_pairs={{0,2},{2,4},{4,6},{6,8},{8,10},{10,12},{12,14},{14,16},{16,18},{18... | collective-permute-start | bytes 1966088 | tf_op jit(solution)/shard_map/ppermute | solution.py:22
  3.9 0.1 dynamic-slice_bitcast_fusion.3
  4.0 0.5 collective-permute-start.2
  4.6 1.2 collective-permute-start
  5.8 2.4 %collective-permute-start.1 = (bf16[160,640]{1,0:T(8,128)(2,1)S(1)}, bf16[160,640]{1,0:T(8,128)(2,1)S(1)}, u32[]{:S(2)}, u32[]{:S(2)}) collective-permute-start(bf16[160,640]{1,0:T(8,128)(2,1)S(1)} %pad_maximum_fusion.5), channel_id=1, source_target_pairs={{0,16},{8,24},{16,0},{24,8},{1,17},{9,25},{17,1},{25,9},{2,18},{10... | collective-permute-start | bytes 614408 | tf_op jit(solution)/shard_map/ppermute | solution.py:26
  8.2 1.5 collective-permute-start.4
  9.7 6.1 %collective-permute-done.2 = bf16[160,640]{1,0:T(8,128)(2,1)S(1)} collective-permute-done((bf16[160,640]{1,0:T(8,128)(2,1)S(1)}, bf16[160,640]{1,0:T(8,128)(2,1)S(1)}, u32[]{:S(2)}, u32[]{:S(2)}) %collective-permute-start.2) | collective-permute-done | bytes 204832 | tf_op jit(solution)/shard_map/ppermute | solution.py:26
  15.8 0.0 collective-permute-start.3
  15.9 0.0 collective-permute-done
  15.9 6.7 %collective-permute-done.1 = bf16[160,640]{1,0:T(8,128)(2,1)S(1)} collective-permute-done((bf16[160,640]{1,0:T(8,128)(2,1)S(1)}, bf16[160,640]{1,0:T(8,128)(2,1)S(1)}, u32[]{:S(2)}, u32[]{:S(2)}) %collective-permute-start.1) | collective-permute-done | bytes 204832 | tf_op jit(solution)/shard_map/ppermute | solution.py:26
  22.6 0.1 pad_maximum_fusion.refs_8_
  22.7 0.0 copy-start.7
  22.8 6.9 %collective-permute-done.3.refs_1_ = bf16[128,1280]{1,0:T(8,128)(2,1)} collective-permute-done((bf16[128,1280]{1,0:T(8,128)(2,1)S(1)}, bf16[128,1280]{1,0:T(8,128)(2,1)}, u32[]{:S(2)}, u32[]{:S(2)}) %collective-permute-start.3) | collective-permute-done | bytes 327712 | tf_op jit(solution)/shard_map/ppermute | solution.py:217
  29.6 10.5 %collective-permute-start.10 = (bf16[4,160,640]{2,1,0:T(8,128)(2,1)S(1)}, bf16[4,160,640]{2,1,0:T(8,128)(2,1)S(1)}, u32[]{:S(2)}, u32[]{:S(2)}) collective-permute-start(bf16[4,160,640]{2,1,0:T(8,128)(2,1)S(1)} %pad_maximum_fusion.refs_8_), channel_id=1, source_target_pairs={{0,2},{2,0},{4,6},{6,4},{1,3},{3,1},{5,7},{7,5},{8,10},{10,8},{12,... | collective-permute-start | bytes 2457608 | tf_op jit(solution)/shard_map/ppermute | solution.py:26
  40.2 1.5 collective-permute-start.9
  41.7 1.0 collective-permute-start.8
  42.7 8.3 %collective-permute-start.14 = (bf16[4,160,640]{2,1,0:T(8,128)(2,1)S(1)}, bf16[4,160,640]{2,1,0:T(8,128)(2,1)S(1)}, u32[]{:S(2)}, u32[]{:S(2)}) collective-permute-start(bf16[4,160,640]{2,1,0:T(8,128)(2,1)S(1)} %collective-permute-done.6.refs_10_), channel_id=1, source_target_pairs={{0,2},{2,0},{4,6},{6,4},{1,3},{3,1},{5,7},{7,5},{8,10},{10,8},{12,... | collective-permute-start | bytes 2457608 | tf_op jit(solution)/shard_map/ppermute | solution.py:26
  51.0 0.3 collective-permute-done.8.refs_2_
  51.3 2.8 %collective-permute-start.11 = (bf16[128,1280]{1,0:T(8,128)(2,1)}, bf16[128,1280]{1,0:T(8,128)(2,1)}, u32[]{:S(2)}, u32[]{:S(2)}) collective-permute-start(bf16[128,1280]{1,0:T(8,128)(2,1)} %collective-permute-done.8.refs_2_), channel_id=1, source_target_pairs={{0,8},{8,24},{24,16},{16,0},{1,9},{9,25},{25,17},{17,1},{2,10},{10... | collective-permute-start | bytes 983048 | tf_op jit(solution)/shard_map/ppermute | solution.py:217
  54.2 1.9 %collective-permute-start.7 = (bf16[2,128,1280]{2,1,0:T(8,128)(2,1)}, bf16[2,128,1280]{2,1,0:T(8,128)(2,1)}, u32[]{:S(2)}, u32[]{:S(2)}) collective-permute-start(bf16[2,128,1280]{2,1,0:T(8,128)(2,1)} %collective-permute-done.5.kv1_ref), channel_id=1, source_target_pairs={{0,2},{2,4},{4,6},{6,8},{8,10},{10,12},{12,14},{14,16},{16,18},{18... | collective-permute-start | bytes 1966088 | tf_op jit(solution)/shard_map/ppermute | solution.py:22
  56.1 0.7 fusion
  56.8 0.7 concatenate.31.order_ref
  57.5 1.6 %collective-permute-start.12 = (bf16[128,1280]{1,0:T(8,128)(2,1)}, bf16[128,1280]{1,0:T(8,128)(2,1)S(1)}, u32[]{:S(2)}, u32[]{:S(2)}) collective-permute-start(bf16[128,1280]{1,0:T(8,128)(2,1)} %collective-permute-done.8.refs_2_), channel_id=1, source_target_pairs={{0,1},{1,0},{2,3},{3,2},{4,5},{5,4},{6,7},{7,6},{8,9},{9,8},{10,11... | collective-permute-start | bytes 983048 | tf_op jit(solution)/shard_map/ppermute | solution.py:26
  59.1 3.4 %collective-permute-done.11.refs_3_ = bf16[128,1280]{1,0:T(8,128)(2,1)} collective-permute-done((bf16[128,1280]{1,0:T(8,128)(2,1)}, bf16[128,1280]{1,0:T(8,128)(2,1)}, u32[]{:S(2)}, u32[]{:S(2)}) %collective-permute-start.11) | collective-permute-done | bytes 327712 | tf_op jit(solution)/shard_map/ppermute | solution.py:217
  62.5 1.5 collective-permute-start.13
  64.0 0.2 convert_reduce_fusion
  64.3 0.6 multiply_add_fusion
  64.9 7.3 %collective-permute-done.7.kv2_ref = bf16[2,128,1280]{2,1,0:T(8,128)(2,1)} collective-permute-done((bf16[2,128,1280]{2,1,0:T(8,128)(2,1)}, bf16[2,128,1280]{2,1,0:T(8,128)(2,1)}, u32[]{:S(2)}, u32[]{:S(2)}) %collective-permute-start.7) | collective-permute-done | bytes 655392 | tf_op jit(solution)/shard_map/ppermute | solution.py:22
  72.2 2.3 %collective-permute-done.13.refs_7_ = bf16[128,1280]{1,0:T(8,128)(2,1)S(1)} collective-permute-done((bf16[128,1280]{1,0:T(8,128)(2,1)}, bf16[128,1280]{1,0:T(8,128)(2,1)S(1)}, u32[]{:S(2)}, u32[]{:S(2)}) %collective-permute-start.13) | collective-permute-done | bytes 327712 | tf_op jit(solution)/shard_map/ppermute | solution.py:26
  74.5 0.7 copy-done.9
  75.2 0.9 copy-done.3
  76.1 5.8 %project.3 = bf16[16,4,16,384]{3,2,1,0:T(8,128)(2,1)} custom-call(s32[14]{0:T(128)} %concatenate.31.order_ref, s32[4,1,128]{2,1,0:T(1,128)} %bitcast.50, bf16[128,1280]{1,0:T(8,128)(2,1)} %refs_0_.3, bf16[128,1280]{1,0:T(8,128)(2,1)} %collective-permute-done.3.refs_1_, bf16[128,1280]{1,0:T(8,128)(2,1)} %collective-permute-done.8.refs_2_, ...), custom_call_target="tpu_custom_call" | custom-call | flops 1006632960 | bytes 8388608 | tf_op jit(solution)/shard_map/project/pallas_call | solution.py:167
  81.9 5.7 %all-to-all-start.1 = ((bf16[16,4,16,384]{3,2,1,0:T(8,128)(2,1)}), bf16[16,4,16,384]{3,2,1,0:T(8,128)(2,1)S(1)}, u32[]{:S(2)}, u32[]{:S(2)}) async-start(bf16[16,4,16,384]{3,2,1,0:T(8,128)(2,1)} %project.3), calls=%async_computation.1 | async-start | bytes 1572864 | tf_op jit(solution)/shard_map/all_to_all | solution.py:295
  87.6 5.1 %project.2 = bf16[16,4,16,256]{3,2,1,0:T(8,128)(2,1)} custom-call(s32[14]{0:T(128)} %concatenate.31.order_ref, s32[4,1,128]{2,1,0:T(1,128)} %bitcast.51, bf16[128,1280]{1,0:T(8,128)(2,1)} %refs_0_.3, bf16[128,1280]{1,0:T(8,128)(2,1)} %collective-permute-done.3.refs_1_, bf16[128,1280]{1,0:T(8,128)(2,1)} %collective-permute-done.8.refs_2_, ...), custom_call_target="tpu_custom_call" | custom-call | flops 671088640 | bytes 8388608 | tf_op jit(solution)/shard_map/project/pallas_call | solution.py:167
  92.7 14.5 %all-to-all-done.1 = bf16[16,4,16,384]{3,2,1,0:T(8,128)(2,1)S(1)} async-done(((bf16[16,4,16,384]{3,2,1,0:T(8,128)(2,1)}), bf16[16,4,16,384]{3,2,1,0:T(8,128)(2,1)S(1)}, u32[]{:S(2)}, u32[]{:S(2)}) %all-to-all-start.1) | async-done | bytes 786464 | tf_op jit(solution)/shard_map/all_to_all | solution.py:295
  107.2 4.6 %all-to-all-start = ((bf16[16,4,16,256]{3,2,1,0:T(8,128)(2,1)}), bf16[16,4,16,256]{3,2,1,0:T(8,128)(2,1)S(1)}, u32[]{:S(2)}, u32[]{:S(2)}) async-start(bf16[16,4,16,256]{3,2,1,0:T(8,128)(2,1)} %project.2), calls=%async_computation | async-start | bytes 1048576 | tf_op jit(solution)/shard_map/all_to_all | solution.py:295
  111.8 0.1 convert_reduce_fusion.1
  111.9 0.0 copy-start.15
  112.0 0.1 copy.16
  112.0 0.1 iota_compare_fusion.1
  112.1 0.1 reshape.64
  112.2 0.4 copy-done.15
  112.6 0.1 dynamic_slice.48
  112.7 0.1 pad_dynamic-slice_fusion
  112.8 0.1 compare_and_fusion
  112.9 0.8 add_select_fusion.bias_ref
  113.7 5.3 %attend.2 = (bf16[128,1280]{1,0:T(8,128)(2,1)}, bf16[128,1280]{1,0:T(8,128)(2,1)}, bf16[2,128,768]{2,1,0:T(8,128)(2,1)}, f32[2,128,768]{2,1,0:T(8,128)}, f32[2,128,768]{2,1,0:T(8,128)}) custom-call(bf16[128,1280]{1,0:T(8,128)(2,1)} %q_ref.3, bf16[128,1280]{1,0:T(8,128)(2,1)} %g_ref.3, bf16[128,1280]{1,0:T(8,128)(2,1)} %k_ref.3, bf16[128,1280]{1,0:T(8,128)(2,1)} %v_ref.3, ...), custom_call_target="tpu_custom_call" | custom-call | flops 629145600 | bytes 8388608 | tf_op jit(solution)/shard_map/attend/pallas_call | solution.py:92
  119.0 6.7 %all-to-all-done = bf16[16,4,16,256]{3,2,1,0:T(8,128)(2,1)S(1)} async-done(((bf16[16,4,16,256]{3,2,1,0:T(8,128)(2,1)}), bf16[16,4,16,256]{3,2,1,0:T(8,128)(2,1)S(1)}, u32[]{:S(2)}, u32[]{:S(2)}) %all-to-all-start) | async-done | bytes 524320 | tf_op jit(solution)/shard_map/all_to_all | solution.py:295
  125.7 0.8 copy-done.5
  126.5 4.8 %attend.3 = (bf16[128,1280]{1,0:T(8,128)(2,1)}, bf16[128,1280]{1,0:T(8,128)(2,1)}, bf16[2,128,512]{2,1,0:T(8,128)(2,1)}, f32[2,128,512]{2,1,0:T(8,128)}, f32[2,128,512]{2,1,0:T(8,128)}) custom-call(bf16[128,1280]{1,0:T(8,128)(2,1)} %q_ref.3, bf16[128,1280]{1,0:T(8,128)(2,1)} %g_ref.3, ...), custom_call_target="tpu_custom_call", output_to_operand_aliasing={{0}: (8, {}), {1}: (9, {})} | custom-call | flops 419430400 | bytes 8388608 | tf_op jit(solution)/shard_map/attend/pallas_call | solution.py:92
  131.3 2.9 %collective-permute-start.17 = (bf16[2,128,512]{2,1,0:T(8,128)(2,1)}, bf16[2,128,512]{2,1,0:T(8,128)(2,1)S(1)}, u32[]{:S(2)}, u32[]{:S(2)}) collective-permute-start(bf16[2,128,512]{2,1,0:T(8,128)(2,1)} %get-tuple-element.45), channel_id=1, source_target_pairs={{2,0},{4,2},{6,4},{8,6},{10,8},{12,10},{14,12},{16,14},{18,16},{20... | collective-permute-start | bytes 786440 | tf_op jit(solution)/shard_map/ppermute | solution.py:22
  134.3 2.1 %collective-permute-start.15 = (bf16[2,128,768]{2,1,0:T(8,128)(2,1)S(1)}, bf16[2,128,768]{2,1,0:T(8,128)(2,1)S(1)}, u32[]{:S(2)}, u32[]{:S(2)}) collective-permute-start(bf16[2,128,768]{2,1,0:T(8,128)(2,1)S(1)} %copy-done.16), channel_id=1, source_target_pairs={{2,0},{4,2},{6,4},{8,6},{10,8},{12,10},{14,12},{16,14},{18,16},{20... | collective-permute-start | bytes 1179656 | tf_op jit(solution)/shard_map/ppermute | solution.py:22
  136.4 2.0 %collective-permute-done.17 = bf16[2,128,512]{2,1,0:T(8,128)(2,1)S(1)} collective-permute-done((bf16[2,128,512]{2,1,0:T(8,128)(2,1)}, bf16[2,128,512]{2,1,0:T(8,128)(2,1)S(1)}, u32[]{:S(2)}, u32[]{:S(2)}) %collective-permute-start.17) | collective-permute-done | bytes 262176 | tf_op jit(solution)/shard_map/ppermute | solution.py:22
  138.4 1.1 add_convert_fusion.3
  139.5 4.6 %collective-permute-start.18 = (bf16[2,128,512]{2,1,0:T(8,128)(2,1)S(1)}, bf16[2,128,512]{2,1,0:T(8,128)(2,1)S(1)}, u32[]{:S(2)}, u32[]{:S(2)}) collective-permute-start(bf16[2,128,512]{2,1,0:T(8,128)(2,1)S(1)} %add_convert_fusion.3), channel_id=1, source_target_pairs={{2,0},{4,2},{6,4},{8,6},{10,8},{12,10},{14,12},{16,14},{18,16},{20... | collective-permute-start | bytes 786440 | tf_op jit(solution)/shard_map/ppermute | solution.py:22
  144.2 0.1 add_convert_fusion.1
  144.3 3.2 %collective-permute-start.16 = (bf16[2,128,768]{2,1,0:T(8,128)(2,1)S(1)}, bf16[2,128,768]{2,1,0:T(8,128)(2,1)S(1)}, u32[]{:S(2)}, u32[]{:S(2)}) collective-permute-start(bf16[2,128,768]{2,1,0:T(8,128)(2,1)S(1)} %add_convert_fusion.1), channel_id=1, source_target_pairs={{2,0},{4,2},{6,4},{8,6},{10,8},{12,10},{14,12},{16,14},{18,16},{20... | collective-permute-start | bytes 1179656 | tf_op jit(solution)/shard_map/ppermute | solution.py:22
  147.5 0.6 collective-permute-done.18
  148.0 0.1 add_convert_fusion.2
  148.1 4.6 %collective-permute-done.16 = bf16[2,128,768]{2,1,0:T(8,128)(2,1)S(1)} collective-permute-done((bf16[2,128,768]{2,1,0:T(8,128)(2,1)S(1)}, bf16[2,128,768]{2,1,0:T(8,128)(2,1)S(1)}, u32[]{:S(2)}, u32[]{:S(2)}) %collective-permute-start.16) | collective-permute-done | bytes 393248 | tf_op jit(solution)/shard_map/ppermute | solution.py:22
  152.7 0.1 add_convert_fusion
  152.9 0.7 pad_maximum_fusion.3
  153.6 0.7 pad_maximum_fusion.2
  (49 shorter events, 0.3 us)
Async XLA Ops:
  0.6 3.2 %copy-start.10 = (bf16[2,160,1280]{2,1,0:T(8,128)(2,1)S(1)}, bf16[2,160,1280]{2,1,0:T(8,128)(2,1)}, u32[]{:S(2)}) copy-start(bf16[2,160,1280]{2,1,0:T(8,128)(2,1)} %param.14) | copy-start | bytes 2457604
  1.9 27.8 %collective-permute-start.5 = (bf16[2,128,1280]{2,1,0:T(8,128)(2,1)S(1)}, bf16[2,128,1280]{2,1,0:T(8,128)(2,1)}, u32[]{:S(2)}, u32[]{:S(2)}) collective-permute-start(bf16[2,128,1280]{2,1,0:T(8,128)(2,1)S(1)} %pad_maximum_fusion.1), channel_id=1, source_target_pairs={{0,2},{2,4},{4,6},{6,8},{8,10},{10,12},{12,14},{14,16},{16,18},{18... | collective-permute-start | bytes 1966088 | tf_op jit(solution)/shard_map/ppermute | solution.py:22
  4.0 11.8 %collective-permute-start.2 = (bf16[160,640]{1,0:T(8,128)(2,1)S(1)}, bf16[160,640]{1,0:T(8,128)(2,1)S(1)}, u32[]{:S(2)}, u32[]{:S(2)}) collective-permute-start(bf16[160,640]{1,0:T(8,128)(2,1)S(1)} %pad_maximum_fusion.6), channel_id=1, source_target_pairs={{0,24},{8,16},{16,8},{24,0},{1,25},{9,17},{17,9},{25,1},{2,26},{10... | collective-permute-start | bytes 614408 | tf_op jit(solution)/shard_map/ppermute | solution.py:26
  4.5 3.7 %copy-start.6 = (bf16[128,1280]{1,0:T(8,128)(2,1)S(1)}, bf16[128,1280]{1,0:T(8,128)(2,1)}, u32[]{:S(2)}) copy-start(bf16[128,1280]{1,0:T(8,128)(2,1)} %refs_0_.3) | copy-start | bytes 983044
  4.6 11.3 %collective-permute-start = (bf16[160,640]{1,0:T(8,128)(2,1)S(1)}, bf16[160,640]{1,0:T(8,128)(2,1)S(1)}, u32[]{:S(2)}, u32[]{:S(2)}) collective-permute-start(bf16[160,640]{1,0:T(8,128)(2,1)S(1)} %pad_maximum_fusion.4), channel_id=1, source_target_pairs={{0,8},{8,0},{16,24},{24,16},{1,9},{9,1},{17,25},{25,17},{2,10},{10... | collective-permute-start | bytes 614408 | tf_op jit(solution)/shard_map/ppermute | solution.py:26
  5.8 16.8 %collective-permute-start.1 = (bf16[160,640]{1,0:T(8,128)(2,1)S(1)}, bf16[160,640]{1,0:T(8,128)(2,1)S(1)}, u32[]{:S(2)}, u32[]{:S(2)}) collective-permute-start(bf16[160,640]{1,0:T(8,128)(2,1)S(1)} %pad_maximum_fusion.5), channel_id=1, source_target_pairs={{0,16},{8,24},{16,0},{24,8},{1,17},{9,25},{17,1},{25,9},{2,18},{10... | collective-permute-start | bytes 614408 | tf_op jit(solution)/shard_map/ppermute | solution.py:26
  8.2 14.5 %collective-permute-start.4 = (bf16[128,1280]{1,0:T(8,128)(2,1)S(1)}, bf16[128,1280]{1,0:T(8,128)(2,1)S(1)}, u32[]{:S(2)}, u32[]{:S(2)}) collective-permute-start(bf16[128,1280]{1,0:T(8,128)(2,1)S(1)} %copy-done.6), channel_id=1, source_target_pairs={{0,1},{1,0},{2,3},{3,2},{4,5},{5,4},{6,7},{7,6},{8,9},{9,8},{10,11... | collective-permute-start | bytes 983048 | tf_op jit(solution)/shard_map/ppermute | solution.py:26
  15.8 13.8 %collective-permute-start.3 = (bf16[128,1280]{1,0:T(8,128)(2,1)S(1)}, bf16[128,1280]{1,0:T(8,128)(2,1)}, u32[]{:S(2)}, u32[]{:S(2)}) collective-permute-start(bf16[128,1280]{1,0:T(8,128)(2,1)S(1)} %copy-done.6), channel_id=1, source_target_pairs={{0,8},{8,24},{24,16},{16,0},{1,9},{9,25},{25,17},{17,1},{2,10},{10... | collective-permute-start | bytes 983048 | tf_op jit(solution)/shard_map/ppermute | solution.py:217
  22.7 52.5 %copy-start = (bf16[4,160,640]{2,1,0:T(8,128)(2,1)}, bf16[4,160,640]{2,1,0:T(8,128)(2,1)S(1)}, u32[]{:S(2)}) copy-start(bf16[4,160,640]{2,1,0:T(8,128)(2,1)S(1)} %pad_maximum_fusion.refs_8_) | copy-start | bytes 2457604
  22.7 19.9 %copy-start.7 = (bf16[128,1280]{1,0:T(8,128)(2,1)}, bf16[128,1280]{1,0:T(8,128)(2,1)S(1)}, u32[]{:S(2)}) copy-start(bf16[128,1280]{1,0:T(8,128)(2,1)S(1)} %collective-permute-done.4.refs_4_) | copy-start | bytes 983044
  29.6 13.0 %collective-permute-start.6 = (bf16[4,160,640]{2,1,0:T(8,128)(2,1)S(1)}, bf16[4,160,640]{2,1,0:T(8,128)(2,1)S(1)}, u32[]{:S(2)}, u32[]{:S(2)}) collective-permute-start(bf16[4,160,640]{2,1,0:T(8,128)(2,1)S(1)} %pad_maximum_fusion.refs_8_), channel_id=1, source_target_pairs={{0,4},{2,6},{4,0},{6,2},{1,5},{3,7},{5,1},{7,3},{8,12},{10,14},{12... | collective-permute-start | bytes 2457608 | tf_op jit(solution)/shard_map/ppermute | solution.py:26
  29.6 21.7 %collective-permute-start.10 = (bf16[4,160,640]{2,1,0:T(8,128)(2,1)S(1)}, bf16[4,160,640]{2,1,0:T(8,128)(2,1)S(1)}, u32[]{:S(2)}, u32[]{:S(2)}) collective-permute-start(bf16[4,160,640]{2,1,0:T(8,128)(2,1)S(1)} %pad_maximum_fusion.refs_8_), channel_id=1, source_target_pairs={{0,2},{2,0},{4,6},{6,4},{1,3},{3,1},{5,7},{7,5},{8,10},{10,8},{12,... | collective-permute-start | bytes 2457608 | tf_op jit(solution)/shard_map/ppermute | solution.py:26
  40.2 10.8 %collective-permute-start.9 = (bf16[128,1280]{1,0:T(8,128)(2,1)}, bf16[128,1280]{1,0:T(8,128)(2,1)}, u32[]{:S(2)}, u32[]{:S(2)}) collective-permute-start(bf16[128,1280]{1,0:T(8,128)(2,1)} %collective-permute-done.3.refs_1_), channel_id=1, source_target_pairs={{0,1},{1,0},{2,3},{3,2},{4,5},{5,4},{6,7},{7,6},{8,9},{9,8},{10,11... | collective-permute-start | bytes 983048 | tf_op jit(solution)/shard_map/ppermute | solution.py:26
  41.7 9.7 %collective-permute-start.8 = (bf16[128,1280]{1,0:T(8,128)(2,1)}, bf16[128,1280]{1,0:T(8,128)(2,1)}, u32[]{:S(2)}, u32[]{:S(2)}) collective-permute-start(bf16[128,1280]{1,0:T(8,128)(2,1)} %collective-permute-done.3.refs_1_), channel_id=1, source_target_pairs={{0,8},{8,24},{24,16},{16,0},{1,9},{9,25},{25,17},{17,1},{2,10},{10... | collective-permute-start | bytes 983048 | tf_op jit(solution)/shard_map/ppermute | solution.py:217
  42.7 32.5 %copy-start.1 = (bf16[4,160,640]{2,1,0:T(8,128)(2,1)}, bf16[4,160,640]{2,1,0:T(8,128)(2,1)S(1)}, u32[]{:S(2)}) copy-start(bf16[4,160,640]{2,1,0:T(8,128)(2,1)S(1)} %collective-permute-done.6.refs_10_) | copy-start | bytes 2457604
  42.7 31.8 %collective-permute-start.14 = (bf16[4,160,640]{2,1,0:T(8,128)(2,1)S(1)}, bf16[4,160,640]{2,1,0:T(8,128)(2,1)S(1)}, u32[]{:S(2)}, u32[]{:S(2)}) collective-permute-start(bf16[4,160,640]{2,1,0:T(8,128)(2,1)S(1)} %collective-permute-done.6.refs_10_), channel_id=1, source_target_pairs={{0,2},{2,0},{4,6},{6,4},{1,3},{3,1},{5,7},{7,5},{8,10},{10,8},{12,... | collective-permute-start | bytes 2457608 | tf_op jit(solution)/shard_map/ppermute | solution.py:26
  51.0 6.5 %copy-start.14 = (s32[2048]{0:T(1024)S(1)}, s32[2048]{0:T(1024)}, u32[]{:S(2)}) copy-start(s32[2048]{0:T(1024)} %param.16) | copy-start | bytes 24580
  51.3 23.9 %copy-start.2 = (bf16[4,160,640]{2,1,0:T(8,128)(2,1)}, bf16[4,160,640]{2,1,0:T(8,128)(2,1)S(1)}, u32[]{:S(2)}) copy-start(bf16[4,160,640]{2,1,0:T(8,128)(2,1)S(1)} %collective-permute-done.10.refs_9_) | copy-start | bytes 2457604
  51.3 11.2 %collective-permute-start.11 = (bf16[128,1280]{1,0:T(8,128)(2,1)}, bf16[128,1280]{1,0:T(8,128)(2,1)}, u32[]{:S(2)}, u32[]{:S(2)}) collective-permute-start(bf16[128,1280]{1,0:T(8,128)(2,1)} %collective-permute-done.8.refs_2_), channel_id=1, source_target_pairs={{0,8},{8,24},{24,16},{16,0},{1,9},{9,25},{25,17},{17,1},{2,10},{10... | collective-permute-start | bytes 983048 | tf_op jit(solution)/shard_map/ppermute | solution.py:217
  54.2 18.0 %collective-permute-start.7 = (bf16[2,128,1280]{2,1,0:T(8,128)(2,1)}, bf16[2,128,1280]{2,1,0:T(8,128)(2,1)}, u32[]{:S(2)}, u32[]{:S(2)}) collective-permute-start(bf16[2,128,1280]{2,1,0:T(8,128)(2,1)} %collective-permute-done.5.kv1_ref), channel_id=1, source_target_pairs={{0,2},{2,4},{4,6},{6,8},{8,10},{10,12},{12,14},{14,16},{16,18},{18... | collective-permute-start | bytes 1966088 | tf_op jit(solution)/shard_map/ppermute | solution.py:22
  57.5 14.7 %collective-permute-start.12 = (bf16[128,1280]{1,0:T(8,128)(2,1)}, bf16[128,1280]{1,0:T(8,128)(2,1)S(1)}, u32[]{:S(2)}, u32[]{:S(2)}) collective-permute-start(bf16[128,1280]{1,0:T(8,128)(2,1)} %collective-permute-done.8.refs_2_), channel_id=1, source_target_pairs={{0,1},{1,0},{2,3},{3,2},{4,5},{5,4},{6,7},{7,6},{8,9},{9,8},{10,11... | collective-permute-start | bytes 983048 | tf_op jit(solution)/shard_map/ppermute | solution.py:26
  62.5 12.0 %collective-permute-start.13 = (bf16[128,1280]{1,0:T(8,128)(2,1)}, bf16[128,1280]{1,0:T(8,128)(2,1)S(1)}, u32[]{:S(2)}, u32[]{:S(2)}) collective-permute-start(bf16[128,1280]{1,0:T(8,128)(2,1)} %collective-permute-done.11.refs_3_), channel_id=1, source_target_pairs={{0,1},{1,0},{2,3},{3,2},{4,5},{5,4},{6,7},{7,6},{8,9},{9,8},{10,11... | collective-permute-start | bytes 983048 | tf_op jit(solution)/shard_map/ppermute | solution.py:26
  72.2 3.0 %copy-start.8 = (bf16[128,1280]{1,0:T(8,128)(2,1)}, bf16[128,1280]{1,0:T(8,128)(2,1)S(1)}, u32[]{:S(2)}) copy-start(bf16[128,1280]{1,0:T(8,128)(2,1)S(1)} %collective-permute-done.12.refs_6_) | copy-start | bytes 983044
  74.5 0.7 copy-start.9
  75.2 0.9 copy-start.3
  81.9 25.3 %all-to-all-start.1 = ((bf16[16,4,16,384]{3,2,1,0:T(8,128)(2,1)}), bf16[16,4,16,384]{3,2,1,0:T(8,128)(2,1)S(1)}, u32[]{:S(2)}, u32[]{:S(2)}) async-start(bf16[16,4,16,384]{3,2,1,0:T(8,128)(2,1)} %project.3), calls=%async_computation.1 | async-start | bytes 1572864 | tf_op jit(solution)/shard_map/all_to_all | solution.py:295
  107.2 6.5 %copy-start.4 = (bf16[16,4,16,384]{3,2,1,0:T(8,128)(2,1)}, bf16[16,4,16,384]{3,2,1,0:T(8,128)(2,1)S(1)}, u32[]{:S(2)}) copy-start(bf16[16,4,16,384]{3,2,1,0:T(8,128)(2,1)S(1)} %all-to-all-done.1) | copy-start | bytes 2359300
  107.2 18.5 %all-to-all-start = ((bf16[16,4,16,256]{3,2,1,0:T(8,128)(2,1)}), bf16[16,4,16,256]{3,2,1,0:T(8,128)(2,1)S(1)}, u32[]{:S(2)}, u32[]{:S(2)}) async-start(bf16[16,4,16,256]{3,2,1,0:T(8,128)(2,1)} %project.2), calls=%async_computation | async-start | bytes 1048576 | tf_op jit(solution)/shard_map/all_to_all | solution.py:295
  111.9 0.7 copy-start.15
  125.7 0.8 copy-start.5
  126.5 7.7 %copy-start.16 = (bf16[2,128,768]{2,1,0:T(8,128)(2,1)S(1)}, bf16[2,128,768]{2,1,0:T(8,128)(2,1)}, u32[]{:S(2)}) copy-start(bf16[2,128,768]{2,1,0:T(8,128)(2,1)} %get-tuple-element.42) | copy-start | bytes 1179652
  131.3 12.9 %copy-start.12 = (f32[2,128,768]{2,1,0:T(8,128)S(1)}, f32[2,128,768]{2,1,0:T(8,128)}, u32[]{:S(2)}) copy-start(f32[2,128,768]{2,1,0:T(8,128)} %get-tuple-element.43) | copy-start | bytes 2359300
  131.3 7.1 %collective-permute-start.17 = (bf16[2,128,512]{2,1,0:T(8,128)(2,1)}, bf16[2,128,512]{2,1,0:T(8,128)(2,1)S(1)}, u32[]{:S(2)}, u32[]{:S(2)}) collective-permute-start(bf16[2,128,512]{2,1,0:T(8,128)(2,1)} %get-tuple-element.45), channel_id=1, source_target_pairs={{2,0},{4,2},{6,4},{8,6},{10,8},{12,10},{14,12},{16,14},{18,16},{20... | collective-permute-start | bytes 786440 | tf_op jit(solution)/shard_map/ppermute | solution.py:22
  134.3 9.9 %collective-permute-start.15 = (bf16[2,128,768]{2,1,0:T(8,128)(2,1)S(1)}, bf16[2,128,768]{2,1,0:T(8,128)(2,1)S(1)}, u32[]{:S(2)}, u32[]{:S(2)}) collective-permute-start(bf16[2,128,768]{2,1,0:T(8,128)(2,1)S(1)} %copy-done.16), channel_id=1, source_target_pairs={{2,0},{4,2},{6,4},{8,6},{10,8},{12,10},{14,12},{16,14},{18,16},{20... | collective-permute-start | bytes 1179656 | tf_op jit(solution)/shard_map/ppermute | solution.py:22
  139.5 8.5 %collective-permute-start.18 = (bf16[2,128,512]{2,1,0:T(8,128)(2,1)S(1)}, bf16[2,128,512]{2,1,0:T(8,128)(2,1)S(1)}, u32[]{:S(2)}, u32[]{:S(2)}) collective-permute-start(bf16[2,128,512]{2,1,0:T(8,128)(2,1)S(1)} %add_convert_fusion.3), channel_id=1, source_target_pairs={{2,0},{4,2},{6,4},{8,6},{10,8},{12,10},{14,12},{16,14},{18,16},{20... | collective-permute-start | bytes 786440 | tf_op jit(solution)/shard_map/ppermute | solution.py:22
  144.2 3.9 %copy-start.13 = (f32[2,128,512]{2,1,0:T(8,128)S(1)}, f32[2,128,512]{2,1,0:T(8,128)}, u32[]{:S(2)}) copy-start(f32[2,128,512]{2,1,0:T(8,128)} %get-tuple-element.47) | copy-start | bytes 1572868
  144.3 8.5 %collective-permute-start.16 = (bf16[2,128,768]{2,1,0:T(8,128)(2,1)S(1)}, bf16[2,128,768]{2,1,0:T(8,128)(2,1)S(1)}, u32[]{:S(2)}, u32[]{:S(2)}) collective-permute-start(bf16[2,128,768]{2,1,0:T(8,128)(2,1)S(1)} %add_convert_fusion.1), channel_id=1, source_target_pairs={{2,0},{4,2},{6,4},{8,6},{10,8},{12,10},{14,12},{16,14},{18,16},{20... | collective-permute-start | bytes 1179656 | tf_op jit(solution)/shard_map/ppermute | solution.py:22
  148.0 4.7 %copy-start.11 = (f32[2,128,768]{2,1,0:T(8,128)S(1)}, f32[2,128,768]{2,1,0:T(8,128)}, u32[]{:S(2)}) copy-start(f32[2,128,768]{2,1,0:T(8,128)} %get-tuple-element.44) | copy-start | bytes 2359300
where the time goes:
time: 157 us; the launch traced here: 154 us
  waiting for transfers between devices  61.5 us (39%)
  starting transfers between devices  60 us (38%)
  Pallas kernels  21 us (13%)
  other arithmetic  6.25 us (4%)
  local copies, waits for them, and re-layouts  4.67 us (3%)
    ppermute x10, starting transfers between devices, swapped(): lax.ppermute(value, axis, [(i, i ^ mask) for i in range(lax.axis_size(axi...  29.1 us
    all_to_all x2, waiting for transfers between devices, body(): lax.all_to_all(part, SEQ, split_axis=0, concat_axis=0, tiled=True)  21.2 us
    ppermute x6, starting transfers between devices, shifted(): return lax.ppermute(value, SEQ, pairs)  16.7 us
    ppermute x10, waiting for transfers between devices, swapped(): lax.ppermute(value, axis, [(i, i ^ mask) for i in range(lax.axis_size(axi...  15.1 us
    ppermute x6, waiting for transfers between devices, shifted(): return lax.ppermute(value, SEQ, pairs)  14.6 us
    pallas_call x2, Pallas kernels, project(): pl.pallas_call(functools.partial(project_kernel, first), in_specs=[pl.Blo...  10.8 us
    ppermute x3, waiting for transfers between devices, ring_step(): lax.ppermute(value, 'z', [(a, b) for a, b in zip(RING, RING[1:] + RING[:1...  10.7 us
    all_to_all x2, starting transfers between devices, body(): lax.all_to_all(part, SEQ, split_axis=0, concat_axis=0, tiled=True)  10.3 us
  transfers between devices with their start and end apart: 21, of which 12 were waited for; matrix products, arithmetic and copies ran while one was open for 3% of the time, Pallas kernels for 7%

commit v1 on v0

--- a/solution.py
+++ b/solution.py
@@ -1,5 +1,3 @@
-import functools
-
 import jax
 import jax.numpy as jnp
 from jax import lax
@@ -13,7 +11,8 @@
 SEQ = ("z", "p")
 ROW_TILE = 16
 RING = [0, 1, 3, 2]
-VMEM = 60 * 1024 * 1024
+VMEM_ATTEND = 60 * 1024 * 1024
+VMEM_PROJECT = 24 * 1024 * 1024
 
 
 def shifted(value, by):
@@ -31,9 +30,9 @@
 
 
 def attend_kernel(
-    q_ref, g_ref, k_ref, v_ref, kv1_ref, kv2_ref, mem_ref, bias_ref, *refs
+    q_ref, g_ref, k_ref, v_ref, kv1_ref, kv2_ref, mem_ref, bias_ref,
+    out_ref, gq_ref, far_ref, near_ref, own_ref,
 ):
-    out_ref, gq_ref, far_ref, near_ref, own_ref = refs[-5:]
     rows, width = q_ref.shape
     slots = mem_ref.shape[1]
     scaling = HD ** (-0.5)
@@ -78,16 +77,13 @@
             own_ref[i, :, cols] = grad[2 * rows :]
 
 
-def attend(first, queries, grad_out, keys, values, kv1, kv2, memory, bias, earlier):
+def attend(queries, grad_out, keys, values, kv1, kv2, memory, bias):
     rows, features = queries.shape
     steps = memory.shape[0] // 2
     slots, block = memory.shape[1:]
     heads = steps * block // HD
-    offset = first // block
-    flat = pl.BlockSpec((rows, block), lambda i: (0, i + offset))
-    pair = pl.BlockSpec((2, rows, block), lambda i: (0, 0, i + offset))
-    grad = pl.BlockSpec((2, rows, block), lambda i: (0, 0, i))
-    whole = pl.BlockSpec(memory_space=pl.ANY)
+    flat = pl.BlockSpec((rows, block), lambda i: (0, i))
+    pair = pl.BlockSpec((2, rows, block), lambda i: (0, 0, i))
     keys_all = slots + 3 * rows
     return pl.pallas_call(
         attend_kernel,
@@ -96,28 +92,26 @@
             flat, flat, flat, flat, pair, pair,
             pl.BlockSpec((2, slots, block), lambda i: (i, 0, 0)),
             pl.BlockSpec((rows, keys_all), lambda i: (0, 0)),
-            *([whole] * len(earlier)),
         ],
-        out_specs=[flat, flat, grad, grad, grad],
+        out_specs=[flat, flat, pair, pair, pair],
         out_shape=[
             jax.ShapeDtypeStruct((rows, features), jnp.bfloat16),
             jax.ShapeDtypeStruct((rows, features), jnp.bfloat16),
-            jax.ShapeDtypeStruct((2, rows, steps * block), jnp.bfloat16),
-            jax.ShapeDtypeStruct((2, rows, steps * block), jnp.float32),
-            jax.ShapeDtypeStruct((2, rows, steps * block), jnp.float32),
+            jax.ShapeDtypeStruct((2, rows, features), jnp.bfloat16),
+            jax.ShapeDtypeStruct((2, rows, features), jnp.float32),
+            jax.ShapeDtypeStruct((2, rows, features), jnp.float32),
         ],
-        input_output_aliases={8 + i: i for i in range(len(earlier))},
-        compiler_params=pltpu.CompilerParams(vmem_limit_bytes=VMEM),
+        compiler_params=pltpu.CompilerParams(vmem_limit_bytes=VMEM_ATTEND),
         cost_estimate=pl.CostEstimate(
             flops=2 * 5 * rows * keys_all * HD * heads,
             bytes_accessed=8 * 1024 * 1024,
             transcendentals=rows * keys_all * heads,
         ),
         name="attend",
-    )(queries, grad_out, keys, values, kv1, kv2, memory, bias, *earlier)
-
-
-def project_kernel(first, order_ref, place_ref, *refs):
+    )(queries, grad_out, keys, values, kv1, kv2, memory, bias)
+
+
+def project_kernel(order_ref, place_ref, *refs):
     n_z = place_ref.shape[0]
     out_ref, w_ref, a_ref, sems = refs[-4:]
     rows = refs[: 2 * n_z]
@@ -135,7 +129,7 @@
         for k in range(n_z):
             copies.append(
                 pltpu.make_async_copy(
-                    pieces[m].at[k, :, pl.ds(first, block)],
+                    pieces[m].at[k],
                     w_ref.at[order_ref[k], order_ref[n_z + m]],
                     sems.at[len(copies)],
                 )
@@ -158,14 +152,14 @@
         out_ref[:, z] = slots.reshape(devices, capacity, block)
 
 
-def project(first, block, order, place, rows, pieces, devices, capacity):
+def project(order, place, rows, pieces, devices, capacity):
     n_z, _, cache_rows = place.shape
     depth = rows[0].shape[1]
     n_p = len(pieces)
-    w_rows = pieces[0].shape[1]
+    _, w_rows, block = pieces[0].shape
     whole = pl.BlockSpec(memory_space=pl.ANY)
     return pl.pallas_call(
-        functools.partial(project_kernel, first),
+        project_kernel,
         in_specs=[
             pl.BlockSpec(memory_space=pltpu.SMEM),
             pl.BlockSpec(memory_space=pltpu.VMEM),
@@ -178,7 +172,7 @@
             pltpu.VMEM((n_z, cache_rows, 2 * depth), jnp.bfloat16),
             pltpu.SemaphoreType.DMA((n_p * n_z + len(rows),)),
         ],
-        compiler_params=pltpu.CompilerParams(vmem_limit_bytes=VMEM),
+        compiler_params=pltpu.CompilerParams(vmem_limit_bytes=VMEM_PROJECT),
         cost_estimate=pl.CostEstimate(
             flops=4 * n_z * cache_rows * depth * block,
             bytes_accessed=8 * 1024 * 1024,
@@ -198,19 +192,11 @@
     return mine * capacity + ranks
 
 
-def widths(features):
-    heads = features // HD // 2
-    first = (heads + 1) // 2
-    return (first * HD, (heads - first) * HD)
-
-
 def column_block(w_kv, target):
-    parts, offset = [], 0
-    for width in widths(w_kv.shape[2]):
-        start = (target & 1, 0, offset + (target >> 1) * width)
-        parts.append(lax.dynamic_slice(w_kv, start, (1, w_kv.shape[1], width))[0])
-        offset += 2 * width
-    return jnp.concatenate(parts, 1)
+    _, w_rows, features = w_kv.shape
+    half = features // (GROUPS // 2)
+    start = (target & 1, 0, (target >> 1) * half)
+    return lax.dynamic_slice(w_kv, start, (1, w_rows, half))[0]
 
 
 def ring_step(value):
@@ -223,20 +209,20 @@
     cache_rows, depth = cache.shape
     _, w_rows, features = w_kv.shape
     z, p, y = lax.axis_index("z"), lax.axis_index("p"), lax.axis_index("head")
-    chunks = widths(features)
     if n_p == 4 and capacity % ROW_TILE == 0 and w_rows % ROW_TILE == 0:
         blocks = [column_block(w_kv, z ^ mask) for mask in range(n_z)]
         own = jnp.stack(
             [blocks[0]] + [swapped(blocks[mask], "z", mask) for mask in range(1, n_z)], 0
         )
-        row1, other0, near = ring_step(cache), swapped(cache, "head", 1), shifted(stream, 1)
-        own, row1, other0, near = lax.optimization_barrier((own, row1, other0, near))
+        row1, other0 = ring_step(cache), swapped(cache, "head", 1)
+        own, row1, other0, stream = lax.optimization_barrier((own, row1, other0, stream))
         across = swapped(own, "p", 2)
         beside = swapped(own, "p", 1)
+        near = shifted(stream, 1)
         row2, other1 = ring_step(row1), swapped(row1, "head", 1)
         row2, other1, beside = lax.optimization_barrier((row2, other1, beside))
         row3, other2 = ring_step(row2), swapped(row2, "head", 1)
-        across, near = lax.optimization_barrier((across, near))
+        across, near, row3, other2 = lax.optimization_barrier((across, near, row3, other2))
         pieces = [own, beside, across, swapped(across, "p", 1)]
         far = shifted(near, 1)
         rows = [cache, row1, row2, row3, other0, other1, other2, swapped(row3, "head", 1)]
@@ -248,11 +234,7 @@
         ).astype(jnp.int32)
         place, near, far = lax.optimization_barrier((place, near, far))
         place = place.reshape(n_z, 1, cache_rows)
-        slots, first = [], 0
-        for width in chunks:
-            slots.append(project(first, width, order, place, rows, pieces, devices, capacity))
-            first += width
-        return slots, near, far
+        return project(order, place, rows, pieces, devices, capacity), near, far
     near = shifted(stream, 1)
     far = shifted(near, 1)
     targets = [column_block(w_kv, jnp.int32(i)) for i in range(n_z)]
@@ -274,8 +256,7 @@
         proj.reshape(n_z, cache_rows, -1),
         preferred_element_type=jnp.float32,
     ).astype(jnp.bfloat16)
-    slots = slots.reshape(n_z, devices, capacity, -1).transpose(1, 0, 2, 3)
-    return [slots[..., : chunks[0]], slots[..., chunks[0] :]], near, far
+    return slots.reshape(n_z, devices, capacity, -1).transpose(1, 0, 2, 3), near, far
 
 
 def body(queries, keys, values, grad_out, cache, w_kv, doc_ids, routes):
@@ -291,12 +272,8 @@
 
     place = slot_places(routes, n_z, n_p, cache_rows, capacity)
     slots, kv1, kv2 = memory_slots(cache, w_kv, place, capacity, jnp.stack([keys, values], 0))
-    memory = [
-        lax.all_to_all(part, SEQ, split_axis=0, concat_axis=0, tiled=True).reshape(
-            n_z, slot_count, part.shape[-1]
-        )
-        for part in slots
-    ]
+    memory = lax.all_to_all(slots, SEQ, split_axis=0, concat_axis=0, tiled=True)
+    memory = memory.reshape(n_z, slot_count, slots.shape[-1])
 
     incoming = jnp.sum(
         (routes.reshape(n_z, n_p, cache_rows) == my_index).astype(jnp.int32), axis=2
@@ -315,18 +292,12 @@
     )
     bias = jnp.where(allowed, 0.0, -1e30).astype(jnp.float32)
 
-    first, earlier, grads = 0, [], []
-    for part in memory:
-        output, grad_q, far, near, own = attend(
-            first, queries, grad_out, keys, values, kv1, kv2, part, bias, earlier
-        )
-        earlier = [output, grad_q]
-        first += 2 * part.shape[-1]
-        near = shifted(far, -1).astype(jnp.float32) + near
-        own = shifted(near.astype(jnp.bfloat16), -1).astype(jnp.float32) + own
-        grads.append(own.astype(jnp.bfloat16))
-    grad_k, grad_v = (jnp.concatenate([part[i] for part in grads], 1) for i in range(2))
-    return (output, grad_q, grad_k, grad_v)
+    output, grad_q, far, near, own = attend(
+        queries, grad_out, keys, values, kv1, kv2, memory, bias
+    )
+    near = shifted(far, -1).astype(jnp.float32) + near
+    own = shifted(near.astype(jnp.bfloat16), -1).astype(jnp.float32) + own
+    return (output, grad_q, own[0].astype(jnp.bfloat16), own[1].astype(jnp.bfloat16))
 
 
 def solution(mesh):

time: 157 us -> 161 us (1.025)
  waiting for transfers between devices: 61.5 us -> 87.1 us
  starting transfers between devices: 60 us -> 36.6 us
  local copies, waits for them, and re-layouts: 4.67 us -> 13.8 us
  Pallas kernels: 21 us -> 16.9 us
  other arithmetic: 6.25 us -> 3.3 us
    ppermute x10, starting transfers between devices: 29.1 us -> 12.3 us  [swapped(): lax.ppermute(value, axis, [(i, i ^ mask) for i in range(lax.axis_size(axi...]
    ppermute x6 -> x4, waiting for transfers between devices: 14.6 us -> 30.9 us  [shifted(): return lax.ppermute(value, SEQ, pairs)]
    all_to_all x2 -> x1, waiting for transfers between devices: 21.2 us -> 29.3 us  [body(): memory = lax.all_to_all(slots, SEQ, split_axis=0, concat_axis=0, tiled=True)]
    unnamed x34, local copies, waits for them, and re-layouts: 2.88 us -> 10.6 us
    ppermute x10, waiting for transfers between devices: 15.1 us -> 21.6 us  [swapped(): lax.ppermute(value, axis, [(i, i ^ mask) for i in range(lax.axis_size(axi...]
    ppermute x3, waiting for transfers between devices: 10.7 us -> 5.23 us  [ring_step(): lax.ppermute(value, 'z', [(a, b) for a, b in zip(RING, RING[1:] + RING[:1...]
    ppermute x6 -> x4, starting transfers between devices: 16.7 us -> 11.8 us  [shifted(): return lax.ppermute(value, SEQ, pairs)]
    pallas_call x2 -> x1, Pallas kernels: 10.1 us -> 6.9 us  [attend(): pl.pallas_call(attend_kernel, grid=(steps,), in_specs=[flat, flat, flat,...]
  transfers between devices with their start and end apart: 21 -> 18, of which waited for: 12 -> 9; matrix products, arithmetic and copies ran while one was open for 3% -> 3% of each run, Pallas kernels for 7% -> 0%
where the time goes in v1:
time: 161 us; the launch traced here: 158 us
  waiting for transfers between devices  87.1 us (54%)
  starting transfers between devices  36.6 us (23%)
  Pallas kernels  16.9 us (10%)
  local copies, waits for them, and re-layouts  13.8 us (9%)
  other arithmetic  3.3 us (2%)
    ppermute x4, waiting for transfers between devices, shifted(): return lax.ppermute(value, SEQ, pairs)  30.9 us
    all_to_all x1, waiting for transfers between devices, body(): memory = lax.all_to_all(slots, SEQ, split_axis=0, concat_axis=0, tiled=True)  29.3 us
    ppermute x10, waiting for transfers between devices, swapped(): lax.ppermute(value, axis, [(i, i ^ mask) for i in range(lax.axis_size(axi...  21.6 us
    ppermute x10, starting transfers between devices, swapped(): lax.ppermute(value, axis, [(i, i ^ mask) for i in range(lax.axis_size(axi...  12.3 us
    ppermute x4, starting transfers between devices, shifted(): return lax.ppermute(value, SEQ, pairs)  11.8 us
    unnamed x34, local copies, waits for them, and re-layouts  10.6 us
    pallas_call x1, Pallas kernels, project(): pl.pallas_call(project_kernel, in_specs=[pl.BlockSpec(memory_space=pltpu....  10 us
    all_to_all x1, starting transfers between devices, body(): memory = lax.all_to_all(slots, SEQ, split_axis=0, concat_axis=0, tiled=True)  7.79 us
  transfers between devices with their start and end apart: 18, of which 9 were waited for; matrix products, arithmetic and copies ran while one was open for 3% of the time, Pallas kernels for 0%

profile of v1, /device:TPU:16, one launch (start us, length us, event | category | flops | bytes accessed | tf_op | source)
XLA Modules:
  0.0 158.5 jit_solution(16838516404726898587)
XLA Ops:
  0.6 0.0 copy-start.13
  0.6 0.0 copy-start.12
  0.7 0.1 collective-permute-start.3
  0.7 1.8 %collective-permute-start.4 = (bf16[128,1280]{1,0:T(8,128)(2,1)}, bf16[128,1280]{1,0:T(8,128)(2,1)S(1)}, u32[]{:S(2)}, u32[]{:S(2)}) collective-permute-start(bf16[128,1280]{1,0:T(8,128)(2,1)} %refs_0_.1), channel_id=1, source_target_pairs={{0,1},{1,0},{2,3},{3,2},{4,5},{5,4},{6,7},{7,6},{8,9},{9,8},{10,11... | collective-permute-start | bytes 983048 | tf_op jit(solution)/shard_map/ppermute | solution.py:25
  2.6 1.3 constant_dynamic-slice_fusion.1
  3.9 2.8 %collective-permute-start.2 = (bf16[160,640]{1,0:T(8,128)(2,1)S(1)}, bf16[160,640]{1,0:T(8,128)(2,1)S(1)}, u32[]{:S(2)}, u32[]{:S(2)}) collective-permute-start(bf16[160,640]{1,0:T(8,128)(2,1)S(1)} %get-tuple-element.44), channel_id=1, source_target_pairs={{0,24},{8,16},{16,8},{24,0},{1,25},{9,17},{17,9},{25,1},{2,26},{10... | collective-permute-start | bytes 614408 | tf_op jit(solution)/shard_map/ppermute | solution.py:25
  6.6 1.3 collective-permute-start.1
  8.0 0.2 collective-permute-start
  8.2 0.1 pad_maximum_fusion.1
  8.3 17.5 %collective-permute-done.2 = bf16[160,640]{1,0:T(8,128)(2,1)S(1)} collective-permute-done((bf16[160,640]{1,0:T(8,128)(2,1)S(1)}, bf16[160,640]{1,0:T(8,128)(2,1)S(1)}, u32[]{:S(2)}, u32[]{:S(2)}) %collective-permute-start.2) | collective-permute-done | bytes 204832 | tf_op jit(solution)/shard_map/ppermute | solution.py:25
  25.7 0.1 pad_maximum_fusion.refs_8_
  25.9 0.0 collective-permute-done.3.refs_1_
  25.9 0.0 collective-permute-done.4.refs_4_
  25.9 0.0 copy-start.3
  25.9 0.7 copy-done.3
  26.6 0.0 collective-permute-start.9
  26.6 1.5 collective-permute-start.5
  28.2 3.4 %collective-permute-start.7 = (bf16[128,1280]{1,0:T(8,128)(2,1)S(1)}, bf16[128,1280]{1,0:T(8,128)(2,1)S(1)}, u32[]{:S(2)}, u32[]{:S(2)}) collective-permute-start(bf16[128,1280]{1,0:T(8,128)(2,1)S(1)} %collective-permute-done.3.refs_1_), channel_id=1, source_target_pairs={{0,8},{8,24},{24,16},{16,0},{1,9},{9,25},{25,17},{17,1},{2,10},{10... | collective-permute-start | bytes 983048 | tf_op jit(solution)/shard_map/ppermute | solution.py:203
  31.5 1.5 collective-permute-start.8
  33.1 0.7 copy-done.1
  33.8 1.9 %collective-permute-start.6 = (bf16[2,128,1280]{2,1,0:T(8,128)(2,1)S(1)}, bf16[2,128,1280]{2,1,0:T(8,128)(2,1)}, u32[]{:S(2)}, u32[]{:S(2)}) collective-permute-start(bf16[2,128,1280]{2,1,0:T(8,128)(2,1)S(1)} %pad_maximum_fusion.1), channel_id=1, source_target_pairs={{0,2},{2,4},{4,6},{6,8},{8,10},{10,12},{12,14},{14,16},{16,18},{18... | collective-permute-start | bytes 1966088 | tf_op jit(solution)/shard_map/ppermute | solution.py:21
  35.7 5.2 %collective-permute-done.7.refs_2_ = bf16[128,1280]{1,0:T(8,128)(2,1)S(1)} collective-permute-done((bf16[128,1280]{1,0:T(8,128)(2,1)S(1)}, bf16[128,1280]{1,0:T(8,128)(2,1)S(1)}, u32[]{:S(2)}, u32[]{:S(2)}) %collective-permute-start.7) | collective-permute-done | bytes 327712 | tf_op jit(solution)/shard_map/ppermute | solution.py:203
  40.9 0.2 collective-permute-done.8.refs_5_
  41.1 0.7 copy-done.7
  41.8 1.2 collective-permute-start.10
  43.0 1.5 collective-permute-start.11
  44.5 0.7 copy-done.5
  45.3 5.1 %collective-permute-done.6.kv1_ref = bf16[2,128,1280]{2,1,0:T(8,128)(2,1)} collective-permute-done((bf16[2,128,1280]{2,1,0:T(8,128)(2,1)S(1)}, bf16[2,128,1280]{2,1,0:T(8,128)(2,1)}, u32[]{:S(2)}, u32[]{:S(2)}) %collective-permute-start.6) | collective-permute-done | bytes 655392 | tf_op jit(solution)/shard_map/ppermute | solution.py:21
  50.4 3.9 %collective-permute-done.5.refs_10_ = bf16[4,160,640]{2,1,0:T(8,128)(2,1)S(1)} collective-permute-done((bf16[4,160,640]{2,1,0:T(8,128)(2,1)S(1)}, bf16[4,160,640]{2,1,0:T(8,128)(2,1)S(1)}, u32[]{:S(2)}, u32[]{:S(2)}) %collective-permute-start.5) | collective-permute-done | bytes 819232 | tf_op jit(solution)/shard_map/ppermute | solution.py:25
  54.3 0.7 copy-done.9
  55.0 2.4 %collective-permute-start.12 = (bf16[2,128,1280]{2,1,0:T(8,128)(2,1)}, bf16[2,128,1280]{2,1,0:T(8,128)(2,1)}, u32[]{:S(2)}, u32[]{:S(2)}) collective-permute-start(bf16[2,128,1280]{2,1,0:T(8,128)(2,1)} %collective-permute-done.6.kv1_ref), channel_id=1, source_target_pairs={{0,2},{2,4},{4,6},{6,8},{8,10},{10,12},{12,14},{14,16},{16,18},{18... | collective-permute-start | bytes 1966088 | tf_op jit(solution)/shard_map/ppermute | solution.py:21
  57.5 0.7 fusion
  58.2 0.1 concatenate.9.order_ref
  58.3 1.6 %collective-permute-start.13 = (bf16[128,1280]{1,0:T(8,128)(2,1)}, bf16[128,1280]{1,0:T(8,128)(2,1)S(1)}, u32[]{:S(2)}, u32[]{:S(2)}) collective-permute-start(bf16[128,1280]{1,0:T(8,128)(2,1)} %collective-permute-done.10.refs_3_), channel_id=1, source_target_pairs={{0,1},{1,0},{2,3},{3,2},{4,5},{5,4},{6,7},{7,6},{8,9},{9,8},{10,11... | collective-permute-start | bytes 983048 | tf_op jit(solution)/shard_map/ppermute | solution.py:25
  59.9 0.2 convert_reduce_fusion
  60.1 9.3 %collective-permute-done.12.kv2_ref = bf16[2,128,1280]{2,1,0:T(8,128)(2,1)} collective-permute-done((bf16[2,128,1280]{2,1,0:T(8,128)(2,1)}, bf16[2,128,1280]{2,1,0:T(8,128)(2,1)}, u32[]{:S(2)}, u32[]{:S(2)}) %collective-permute-start.12) | collective-permute-done | bytes 655392 | tf_op jit(solution)/shard_map/ppermute | solution.py:21
  69.5 1.0 copy-done
  70.4 1.0 copy-done.2
  71.4 1.0 copy-done.4
  72.4 1.0 copy-done.6
  73.4 1.0 copy-done.8
  74.3 1.0 copy-done.10
  75.3 10.0 %project.1 = bf16[16,4,16,640]{3,2,1,0:T(8,128)(2,1)} custom-call(s32[14]{0:T(128)S(1)} %concatenate.9.order_ref, s32[4,1,128]{2,1,0:T(1,128)S(1)} %bitcast.24, bf16[128,1280]{1,0:T(8,128)(2,1)S(1)} %copy-done, bf16[128,1280]{1,0:T(8,128)(2,1)S(1)} %copy-done.2, bf16[128,1280]{1,0:T(8,128)(2,1)S(1)} %copy-done.6, ...), custom_call_target="tpu_custom_call" | custom-call | flops 1677721600 | bytes 8388608 | tf_op jit(solution)/shard_map/project/pallas_call | solution.py:161
  85.4 0.0 copy-start.16
  85.4 7.8 %all-to-all-start = ((bf16[16,4,16,640]{3,2,1,0:T(8,128)(2,1)}), bf16[16,4,16,640]{3,2,1,0:T(8,128)(2,1)S(1)}, u32[]{:S(2)}, u32[]{:S(2)}) async-start(bf16[16,4,16,640]{3,2,1,0:T(8,128)(2,1)} %project.1), calls=%async_computation | async-start | bytes 2621440 | tf_op jit(solution)/shard_map/all_to_all | solution.py:275
  93.2 0.1 convert_reduce_fusion.1
  93.3 0.1 copy.14
  93.4 0.1 iota_compare_fusion.1
  93.5 0.1 reshape.62
  93.6 0.0 copy-done.16
  93.6 0.1 dynamic_slice.32
  93.7 0.1 pad_dynamic-slice_fusion
  93.7 0.1 compare_and_fusion
  93.9 0.8 add_select_fusion.bias_ref
  94.6 29.3 %all-to-all-done = bf16[16,4,16,640]{3,2,1,0:T(8,128)(2,1)S(1)} async-done(((bf16[16,4,16,640]{3,2,1,0:T(8,128)(2,1)}), bf16[16,4,16,640]{3,2,1,0:T(8,128)(2,1)S(1)}, u32[]{:S(2)}, u32[]{:S(2)}) %all-to-all-start) | async-done | bytes 1310752 | tf_op jit(solution)/shard_map/all_to_all | solution.py:275
  124.0 1.1 copy-done.11
  125.0 6.9 %attend.1 = (bf16[128,1280]{1,0:T(8,128)(2,1)}, bf16[128,1280]{1,0:T(8,128)(2,1)}, bf16[2,128,1280]{2,1,0:T(8,128)(2,1)}, f32[2,128,1280]{2,1,0:T(8,128)}, f32[2,128,1280]{2,1,0:T(8,128)}) custom-call(bf16[128,1280]{1,0:T(8,128)(2,1)} %q_ref.1, bf16[128,1280]{1,0:T(8,128)(2,1)} %g_ref.1, bf16[128,1280]{1,0:T(8,128)(2,1)} %k_ref.1, bf16[128,1280]{1,0:T(8,128)(2,1)} %v_ref.1, ...), custom_call_target="tpu_custom_call" | custom-call | flops 1048576000 | bytes 8388608 | tf_op jit(solution)/shard_map/attend/pallas_call | solution.py:88
  131.9 2.9 %collective-permute-start.15 = (bf16[2,128,1280]{2,1,0:T(8,128)(2,1)}, bf16[2,128,1280]{2,1,0:T(8,128)(2,1)S(1)}, u32[]{:S(2)}, u32[]{:S(2)}) collective-permute-start(bf16[2,128,1280]{2,1,0:T(8,128)(2,1)} %get-tuple-element.39), channel_id=1, source_target_pairs={{2,0},{4,2},{6,4},{8,6},{10,8},{12,10},{14,12},{16,14},{18,16},{20... | collective-permute-start | bytes 1966088 | tf_op jit(solution)/shard_map/ppermute | solution.py:21
  134.8 8.4 %collective-permute-done.15 = bf16[2,128,1280]{2,1,0:T(8,128)(2,1)S(1)} collective-permute-done((bf16[2,128,1280]{2,1,0:T(8,128)(2,1)}, bf16[2,128,1280]{2,1,0:T(8,128)(2,1)S(1)}, u32[]{:S(2)}, u32[]{:S(2)}) %collective-permute-start.15) | collective-permute-done | bytes 655392 | tf_op jit(solution)/shard_map/ppermute | solution.py:21
  143.2 1.6 add_convert_fusion.1
  144.8 4.6 %collective-permute-start.16 = (bf16[2,128,1280]{2,1,0:T(8,128)(2,1)S(1)}, bf16[2,128,1280]{2,1,0:T(8,128)(2,1)S(1)}, u32[]{:S(2)}, u32[]{:S(2)}) collective-permute-start(bf16[2,128,1280]{2,1,0:T(8,128)(2,1)S(1)} %add_convert_fusion.1), channel_id=1, source_target_pairs={{2,0},{4,2},{6,4},{8,6},{10,8},{12,10},{14,12},{16,14},{18,16},{20... | collective-permute-start | bytes 1966088 | tf_op jit(solution)/shard_map/ppermute | solution.py:21
  149.4 8.1 %collective-permute-done.16 = bf16[2,128,1280]{2,1,0:T(8,128)(2,1)S(1)} collective-permute-done((bf16[2,128,1280]{2,1,0:T(8,128)(2,1)S(1)}, bf16[2,128,1280]{2,1,0:T(8,128)(2,1)S(1)}, u32[]{:S(2)}, u32[]{:S(2)}) %collective-permute-start.16) | collective-permute-done | bytes 655392 | tf_op jit(solution)/shard_map/ppermute | solution.py:21
  157.5 0.1 add_convert_fusion
  157.6 0.9 slice_bitcast_fusion
  (31 shorter events, 0.1 us)
Async XLA Ops:
  0.6 7.6 %copy-start.13 = (bf16[128,1280]{1,0:T(8,128)(2,1)S(1)}, bf16[128,1280]{1,0:T(8,128)(2,1)}, u32[]{:S(2)}) copy-start(bf16[128,1280]{1,0:T(8,128)(2,1)} %v_ref.1) | copy-start | bytes 983044
  0.6 7.5 %copy-start.12 = (bf16[128,1280]{1,0:T(8,128)(2,1)S(1)}, bf16[128,1280]{1,0:T(8,128)(2,1)}, u32[]{:S(2)}) copy-start(bf16[128,1280]{1,0:T(8,128)(2,1)} %k_ref.1) | copy-start | bytes 983044
  0.7 25.2 %collective-permute-start.3 = (bf16[128,1280]{1,0:T(8,128)(2,1)}, bf16[128,1280]{1,0:T(8,128)(2,1)S(1)}, u32[]{:S(2)}, u32[]{:S(2)}) collective-permute-start(bf16[128,1280]{1,0:T(8,128)(2,1)} %refs_0_.1), channel_id=1, source_target_pairs={{0,8},{8,24},{24,16},{16,0},{1,9},{9,25},{25,17},{17,1},{2,10},{10... | collective-permute-start | bytes 983048 | tf_op jit(solution)/shard_map/ppermute | solution.py:203
  0.7 25.2 %collective-permute-start.4 = (bf16[128,1280]{1,0:T(8,128)(2,1)}, bf16[128,1280]{1,0:T(8,128)(2,1)S(1)}, u32[]{:S(2)}, u32[]{:S(2)}) collective-permute-start(bf16[128,1280]{1,0:T(8,128)(2,1)} %refs_0_.1), channel_id=1, source_target_pairs={{0,1},{1,0},{2,3},{3,2},{4,5},{5,4},{6,7},{7,6},{8,9},{9,8},{10,11... | collective-permute-start | bytes 983048 | tf_op jit(solution)/shard_map/ppermute | solution.py:25
  3.9 21.9 %collective-permute-start.2 = (bf16[160,640]{1,0:T(8,128)(2,1)S(1)}, bf16[160,640]{1,0:T(8,128)(2,1)S(1)}, u32[]{:S(2)}, u32[]{:S(2)}) collective-permute-start(bf16[160,640]{1,0:T(8,128)(2,1)S(1)} %get-tuple-element.44), channel_id=1, source_target_pairs={{0,24},{8,16},{16,8},{24,0},{1,25},{9,17},{17,9},{25,1},{2,26},{10... | collective-permute-start | bytes 614408 | tf_op jit(solution)/shard_map/ppermute | solution.py:25
  6.6 19.1 %collective-permute-start.1 = (bf16[160,640]{1,0:T(8,128)(2,1)S(1)}, bf16[160,640]{1,0:T(8,128)(2,1)S(1)}, u32[]{:S(2)}, u32[]{:S(2)}) collective-permute-start(bf16[160,640]{1,0:T(8,128)(2,1)S(1)} %get-tuple-element.45), channel_id=1, source_target_pairs={{0,16},{8,24},{16,0},{24,8},{1,17},{9,25},{17,1},{25,9},{2,18},{10... | collective-permute-start | bytes 614408 | tf_op jit(solution)/shard_map/ppermute | solution.py:25
  8.0 17.8 %collective-permute-start = (bf16[160,640]{1,0:T(8,128)(2,1)S(1)}, bf16[160,640]{1,0:T(8,128)(2,1)S(1)}, u32[]{:S(2)}, u32[]{:S(2)}) collective-permute-start(bf16[160,640]{1,0:T(8,128)(2,1)S(1)} %get-tuple-element.43), channel_id=1, source_target_pairs={{0,8},{8,0},{16,24},{24,16},{1,9},{9,1},{17,25},{25,17},{2,10},{10... | collective-permute-start | bytes 614408 | tf_op jit(solution)/shard_map/ppermute | solution.py:25
  8.2 50.0 %copy-start.15 = (s32[2048]{0:T(1024)S(1)}, s32[2048]{0:T(1024)}, u32[]{:S(2)}) copy-start(s32[2048]{0:T(1024)} %param.16) | copy-start | bytes 24580
  25.9 0.7 copy-start.3
  26.6 15.2 %collective-permute-start.9 = (bf16[4,160,640]{2,1,0:T(8,128)(2,1)S(1)}, bf16[4,160,640]{2,1,0:T(8,128)(2,1)S(1)}, u32[]{:S(2)}, u32[]{:S(2)}) collective-permute-start(bf16[4,160,640]{2,1,0:T(8,128)(2,1)S(1)} %pad_maximum_fusion.refs_8_), channel_id=1, source_target_pairs={{0,2},{2,0},{4,6},{6,4},{1,3},{3,1},{5,7},{7,5},{8,10},{10,8},{12,... | collective-permute-start | bytes 2457608 | tf_op jit(solution)/shard_map/ppermute | solution.py:25
  26.6 27.7 %collective-permute-start.5 = (bf16[4,160,640]{2,1,0:T(8,128)(2,1)S(1)}, bf16[4,160,640]{2,1,0:T(8,128)(2,1)S(1)}, u32[]{:S(2)}, u32[]{:S(2)}) collective-permute-start(bf16[4,160,640]{2,1,0:T(8,128)(2,1)S(1)} %pad_maximum_fusion.refs_8_), channel_id=1, source_target_pairs={{0,4},{2,6},{4,0},{6,2},{1,5},{3,7},{5,1},{7,3},{8,12},{10,14},{12... | collective-permute-start | bytes 2457608 | tf_op jit(solution)/shard_map/ppermute | solution.py:25
  28.2 12.8 %collective-permute-start.7 = (bf16[128,1280]{1,0:T(8,128)(2,1)S(1)}, bf16[128,1280]{1,0:T(8,128)(2,1)S(1)}, u32[]{:S(2)}, u32[]{:S(2)}) collective-permute-start(bf16[128,1280]{1,0:T(8,128)(2,1)S(1)} %collective-permute-done.3.refs_1_), channel_id=1, source_target_pairs={{0,8},{8,24},{24,16},{16,0},{1,9},{9,25},{25,17},{17,1},{2,10},{10... | collective-permute-start | bytes 983048 | tf_op jit(solution)/shard_map/ppermute | solution.py:203
  31.5 9.6 %collective-permute-start.8 = (bf16[128,1280]{1,0:T(8,128)(2,1)S(1)}, bf16[128,1280]{1,0:T(8,128)(2,1)S(1)}, u32[]{:S(2)}, u32[]{:S(2)}) collective-permute-start(bf16[128,1280]{1,0:T(8,128)(2,1)S(1)} %collective-permute-done.3.refs_1_), channel_id=1, source_target_pairs={{0,1},{1,0},{2,3},{3,2},{4,5},{5,4},{6,7},{7,6},{8,9},{9,8},{10,11... | collective-permute-start | bytes 983048 | tf_op jit(solution)/shard_map/ppermute | solution.py:25
  33.1 0.7 copy-start.1
  33.8 16.6 %collective-permute-start.6 = (bf16[2,128,1280]{2,1,0:T(8,128)(2,1)S(1)}, bf16[2,128,1280]{2,1,0:T(8,128)(2,1)}, u32[]{:S(2)}, u32[]{:S(2)}) collective-permute-start(bf16[2,128,1280]{2,1,0:T(8,128)(2,1)S(1)} %pad_maximum_fusion.1), channel_id=1, source_target_pairs={{0,2},{2,4},{4,6},{6,8},{8,10},{10,12},{12,14},{14,16},{16,18},{18... | collective-permute-start | bytes 1966088 | tf_op jit(solution)/shard_map/ppermute | solution.py:21
  41.1 0.7 copy-start.7
  41.8 12.5 %collective-permute-start.10 = (bf16[128,1280]{1,0:T(8,128)(2,1)S(1)}, bf16[128,1280]{1,0:T(8,128)(2,1)}, u32[]{:S(2)}, u32[]{:S(2)}) collective-permute-start(bf16[128,1280]{1,0:T(8,128)(2,1)S(1)} %collective-permute-done.7.refs_2_), channel_id=1, source_target_pairs={{0,8},{8,24},{24,16},{16,0},{1,9},{9,25},{25,17},{17,1},{2,10},{10... | collective-permute-start | bytes 983048 | tf_op jit(solution)/shard_map/ppermute | solution.py:203
  43.0 11.3 %collective-permute-start.11 = (bf16[128,1280]{1,0:T(8,128)(2,1)S(1)}, bf16[128,1280]{1,0:T(8,128)(2,1)S(1)}, u32[]{:S(2)}, u32[]{:S(2)}) collective-permute-start(bf16[128,1280]{1,0:T(8,128)(2,1)S(1)} %collective-permute-done.7.refs_2_), channel_id=1, source_target_pairs={{0,1},{1,0},{2,3},{3,2},{4,5},{5,4},{6,7},{7,6},{8,9},{9,8},{10,11... | collective-permute-start | bytes 983048 | tf_op jit(solution)/shard_map/ppermute | solution.py:25
  44.5 0.7 copy-start.5
  54.3 0.7 copy-start.9
  55.0 14.4 %collective-permute-start.14 = (bf16[4,160,640]{2,1,0:T(8,128)(2,1)S(1)}, bf16[4,160,640]{2,1,0:T(8,128)(2,1)S(1)}, u32[]{:S(2)}, u32[]{:S(2)}) collective-permute-start(bf16[4,160,640]{2,1,0:T(8,128)(2,1)S(1)} %collective-permute-done.5.refs_10_), channel_id=1, source_target_pairs={{0,2},{2,0},{4,6},{6,4},{1,3},{3,1},{5,7},{7,5},{8,10},{10,8},{12,... | collective-permute-start | bytes 2457608 | tf_op jit(solution)/shard_map/ppermute | solution.py:25
  55.0 14.4 %collective-permute-start.12 = (bf16[2,128,1280]{2,1,0:T(8,128)(2,1)}, bf16[2,128,1280]{2,1,0:T(8,128)(2,1)}, u32[]{:S(2)}, u32[]{:S(2)}) collective-permute-start(bf16[2,128,1280]{2,1,0:T(8,128)(2,1)} %collective-permute-done.6.kv1_ref), channel_id=1, source_target_pairs={{0,2},{2,4},{4,6},{6,8},{8,10},{10,12},{12,14},{14,16},{16,18},{18... | collective-permute-start | bytes 1966088 | tf_op jit(solution)/shard_map/ppermute | solution.py:21
  58.3 11.2 %collective-permute-start.13 = (bf16[128,1280]{1,0:T(8,128)(2,1)}, bf16[128,1280]{1,0:T(8,128)(2,1)S(1)}, u32[]{:S(2)}, u32[]{:S(2)}) collective-permute-start(bf16[128,1280]{1,0:T(8,128)(2,1)} %collective-permute-done.10.refs_3_), channel_id=1, source_target_pairs={{0,1},{1,0},{2,3},{3,2},{4,5},{5,4},{6,7},{7,6},{8,9},{9,8},{10,11... | collective-permute-start | bytes 983048 | tf_op jit(solution)/shard_map/ppermute | solution.py:25
  69.5 1.0 copy-start
  70.4 1.0 copy-start.2
  71.4 1.0 copy-start.4
  72.4 1.0 copy-start.6
  73.4 1.0 copy-start.8
  74.3 1.0 copy-start.10
  85.4 8.2 %copy-start.16 = (s32[2048]{0:T(1024)S(1)}, s32[2048]{0:T(1024)}, u32[]{:S(2)}) copy-start(s32[2048]{0:T(1024)} %param.15) | copy-start | bytes 24580
  85.4 38.6 %all-to-all-start = ((bf16[16,4,16,640]{3,2,1,0:T(8,128)(2,1)}), bf16[16,4,16,640]{3,2,1,0:T(8,128)(2,1)S(1)}, u32[]{:S(2)}, u32[]{:S(2)}) async-start(bf16[16,4,16,640]{3,2,1,0:T(8,128)(2,1)} %project.1), calls=%async_computation | async-start | bytes 2621440 | tf_op jit(solution)/shard_map/all_to_all | solution.py:275
  124.0 1.1 copy-start.11
  131.9 11.3 %collective-permute-start.15 = (bf16[2,128,1280]{2,1,0:T(8,128)(2,1)}, bf16[2,128,1280]{2,1,0:T(8,128)(2,1)S(1)}, u32[]{:S(2)}, u32[]{:S(2)}) collective-permute-start(bf16[2,128,1280]{2,1,0:T(8,128)(2,1)} %get-tuple-element.39), channel_id=1, source_target_pairs={{2,0},{4,2},{6,4},{8,6},{10,8},{12,10},{14,12},{16,14},{18,16},{20... | collective-permute-start | bytes 1966088 | tf_op jit(solution)/shard_map/ppermute | solution.py:21
  143.2 14.3 %copy-start.14 = (f32[2,128,1280]{2,1,0:T(8,128)S(1)}, f32[2,128,1280]{2,1,0:T(8,128)}, u32[]{:S(2)}) copy-start(f32[2,128,1280]{2,1,0:T(8,128)} %get-tuple-element.41) | copy-start | bytes 3932164
  144.8 12.7 %collective-permute-start.16 = (bf16[2,128,1280]{2,1,0:T(8,128)(2,1)S(1)}, bf16[2,128,1280]{2,1,0:T(8,128)(2,1)S(1)}, u32[]{:S(2)}, u32[]{:S(2)}) collective-permute-start(bf16[2,128,1280]{2,1,0:T(8,128)(2,1)S(1)} %add_convert_fusion.1), channel_id=1, source_target_pairs={{2,0},{4,2},{6,4},{8,6},{10,8},{12,10},{14,12},{16,14},{18,16},{20... | collective-permute-start | bytes 1966088 | tf_op jit(solution)/shard_map/ppermute | solution.py:21
